TPU v7x, 256 devices: a whole 4x4x8 slice. The times are simulated.
256 devices in a mesh: ctx: 256 (over z, x, y, core).
Axes of the slice: x: 4, y: 4, z: 8, core: 2. Of those that a mesh axis runs over, the one named last changes fastest.
Arguments:
- projected: bfloat16 [3, 32768, 512], P(None, 'ctx'), may hold values from -6 to 6
- short_taps: float32 [3, 3, 512], replicated, may hold values from -3.5 to 3.5
- long_filter: float32 [32768, 512], P('ctx'), may hold values from -0.03125 to 0.03125
- skip_weight: float32 [512], replicated, may hold values from -4 to 4
Outputs:
- gated: bfloat16 [32768, 512], P('ctx')
All inputs are finite; a program needn't handle non-finite values.
Results may differ from a plain program's by a relative error of at most 0.0012.
Values may be sent and summed in bfloat16 or wider, within the bound.
A program may use at most 64 MiB of HBM per device.

v0:
```python
import math

import jax
import jax.numpy as jnp
from jax import lax
from jax.sharding import PartitionSpec as P


def shifted(value, axis, by):
    size = lax.axis_size(axis)
    pairs = [(i, i + by) for i in range(size) if 0 <= i + by < size]
    return lax.ppermute(value, axis, pairs)


def from_partner(block, axis, apart):
    count = lax.axis_size(axis)
    route = []
    for low in range(count):
        high = low | 1 << apart
        if high != low and high < count:
            route += [(low, high), (high, low)]
    return lax.ppermute(block, axis, route)


def complex_scale(paired, scale_re, scale_im):
    return jnp.stack(
        [paired[0] * scale_re - paired[1] * scale_im, paired[0] * scale_im + paired[1] * scale_re]
    )


def section_factors(device_index, level, conjugate):
    upper_flag = device_index >> level & 1
    offset = device_index & (1 << level) - 1
    angle = -math.pi * offset.astype(jnp.float32) / float(1 << level)
    sign_flip = 1.0 - 2.0 * upper_flag.astype(jnp.float32)
    twiddle_re = jnp.where(upper_flag == 1, jnp.cos(angle), 1.0)
    twiddle_im = jnp.where(upper_flag == 1, jnp.sin(angle), 0.0)
    if conjugate:
        twiddle_im = -twiddle_im
    return (sign_flip, twiddle_re, twiddle_im)


def forward_step(current, received, factors):
    return complex_scale(factors[0] * current + received, factors[1], factors[2])


def two_streams(signal, cos_pos, sin_pos):
    zeros_part = jnp.zeros_like(signal)
    return jnp.stack(
        [jnp.stack([signal, signal * cos_pos]), jnp.stack([zeros_part, -signal * sin_pos])]
    )


def apply_forward(matrix, part):
    return jnp.einsum("rk,src->skc", matrix, part, precision=lax.Precision.HIGHEST)


def apply_inverse(matrix, part):
    return jnp.einsum("rk,skc->src", matrix, part, precision=lax.Precision.HIGHEST)


def spectral(matrix_re, matrix_im, signal):
    return jnp.stack(
        [
            apply_forward(matrix_re, signal[0]) - apply_forward(matrix_im, signal[1]),
            apply_forward(matrix_re, signal[1]) + apply_forward(matrix_im, signal[0]),
        ]
    )


def unspectral(matrix_re, matrix_im, signal):
    return jnp.stack(
        [
            apply_inverse(matrix_re, signal[0]) + apply_inverse(matrix_im, signal[1]),
            apply_inverse(matrix_re, signal[1]) - apply_inverse(matrix_im, signal[0]),
        ]
    )


def per_device(projected, short_taps, long_filter, skip_weight):
    device_count = lax.axis_size("ctx")
    device_index = lax.axis_index("ctx")
    sections = device_count.bit_length() - 1
    local_rows = projected.shape[1]
    total_rows = local_rows * device_count
    rim_rows = shifted(projected[:, local_rows - 2 :, :], "ctx", 1)
    extended = jnp.concatenate([rim_rows, projected], axis=1).astype(jnp.float32)
    shorted = (
        short_taps[:, 0, None, :] * extended[:, 2:, :]
        + short_taps[:, 1, None, :] * extended[:, 1:-1, :]
        + short_taps[:, 2, None, :] * extended[:, :-2, :]
    )
    mixed_in = shorted[1] * shorted[2]
    positions = device_index * local_rows + lax.iota(jnp.int32, local_rows)
    angle = math.pi * positions.astype(jnp.float32) / float(total_rows)
    own_cos = jnp.cos(angle)[:, None]
    own_sin = jnp.sin(angle)[:, None]
    data_streams = two_streams(mixed_in, own_cos, own_sin)
    filter_streams = two_streams(long_filter, own_cos, own_sin)
    freq_base = jnp.zeros((), jnp.int32)
    for level in range(sections):
        freq_base = freq_base + (device_index >> level & 1) * (1 << sections - 1 - level)
    time_index = lax.iota(jnp.int32, local_rows)[:, None]
    freq_index = freq_base + device_count * lax.iota(jnp.int32, local_rows)[None, :]
    phase = time_index * freq_index % total_rows
    matrix_angle = -2.0 * math.pi * phase.astype(jnp.float32) / float(total_rows)
    matrix_re = jnp.cos(matrix_angle)
    matrix_im = jnp.sin(matrix_angle)
    for level in reversed(range(sections)):
        received = from_partner(data_streams, "ctx", level)
        data_streams = forward_step(
            data_streams, received, section_factors(device_index, level, False)
        )
    for level in reversed(range(sections)):
        received = from_partner(filter_streams, "ctx", level)
        filter_streams = forward_step(
            filter_streams, received, section_factors(device_index, level, False)
        )
    data_spec = spectral(matrix_re, matrix_im, data_streams)
    filter_spec = spectral(matrix_re, matrix_im, filter_streams)
    product = jnp.stack(
        [
            data_spec[0] * filter_spec[0] - data_spec[1] * filter_spec[1],
            data_spec[0] * filter_spec[1] + data_spec[1] * filter_spec[0],
        ]
    )
    inverse = unspectral(matrix_re, matrix_im, product)
    for level in range(sections - 1):
        factors = section_factors(device_index, level, True)
        sent = complex_scale(inverse, factors[1], factors[2])
        received = from_partner(sent, "ctx", level)
        inverse = factors[0] * sent + received
    last_level = sections - 1
    sign_flip, twiddle_re, twiddle_im = section_factors(device_index, last_level, True)
    sent = complex_scale(inverse, twiddle_re, twiddle_im)
    received = from_partner(sent, "ctx", last_level)
    final_values = sign_flip * sent + received
    convolved = (
        final_values[0, 0] + own_cos * final_values[0, 1] - own_sin * final_values[1, 1]
    ) / float(2 * total_rows)
    gated = shorted[0] * (convolved + skip_weight * mixed_in)
    return gated.astype(jnp.bfloat16)


def solution(mesh):
    return jax.shard_map(
        per_device,
        mesh=mesh,
        in_specs=(P(None, "ctx", None), P(), P("ctx", None), P()),
        out_specs=P("ctx", None),
        check_vma=False,
    )
```

profile of v0, /device:TPU:1, one launch (start us, length us, event | category | flops | bytes accessed | tf_op | source)
XLA Modules:
  0.0 620.4 jit_solution(18034579266661632683)
XLA Ops:
  1.4 7.8 %collective-permute-start.9 = (f32[2,2,128,512]{2,3,1,0:T(8,128)S(1)}, f32[2,2,128,512]{2,3,1,0:T(8,128)}, u32[]{:S(2)}, u32[]{:S(2)}) collective-permute-start(f32[2,2,128,512]{2,3,1,0:T(8,128)S(1)} %pad_maximum_fusion.8), channel_id=1, source_target_pairs={{0,128},{128,0},{1,129},{129,1},{2,130},{130,2},{3,131},{131,3},{4... | collective-permute-start | bytes 3145736 | tf_op jit(solution)/shard_map/ppermute | solution.py:22
  10.3 4.0 collective-permute-start
  14.8 4.6 collective-permute-done
  23.4 14.3 %collective-permute-done.9 = f32[2,2,128,512]{2,3,1,0:T(8,128)} collective-permute-done((f32[2,2,128,512]{2,3,1,0:T(8,128)S(1)}, f32[2,2,128,512]{2,3,1,0:T(8,128)}, u32[]{:S(2)}, u32[]{:S(2)}) %collective-permute-start.9) | collective-permute-done | bytes 1048608 | tf_op jit(solution)/shard_map/ppermute | solution.py:22
  37.7 1.3 multiply_add_fusion.15
  40.2 29.8 %collective-permute-start.10 = (f32[2,2,128,512]{2,3,1,0:T(8,128)}, f32[2,2,128,512]{2,3,1,0:T(8,128)}, u32[]{:S(2)}, u32[]{:S(2)}) collective-permute-start(f32[2,2,128,512]{2,3,1,0:T(8,128)} %pad_maximum_fusion.9), channel_id=1, source_target_pairs={{0,64},{64,0},{1,65},{65,1},{2,66},{66,2},{3,67},{67,3},{4,68},{68... | collective-permute-start | bytes 3145736 | tf_op jit(solution)/shard_map/ppermute | solution.py:22
  70.2 6.8 %collective-permute-done.1 = f32[2,2,128,512]{2,3,1,0:T(8,128)} collective-permute-done((f32[2,2,128,512]{2,3,1,0:T(8,128)}, f32[2,2,128,512]{2,3,1,0:T(8,128)}, u32[]{:S(2)}, u32[]{:S(2)}) %collective-permute-start.1) | collective-permute-done | bytes 1048608 | tf_op jit(solution)/shard_map/ppermute | solution.py:22
  79.5 2.8 collective-permute-start.2
  82.3 86.3 %collective-permute-done.10 = f32[2,2,128,512]{2,3,1,0:T(8,128)} collective-permute-done((f32[2,2,128,512]{2,3,1,0:T(8,128)}, f32[2,2,128,512]{2,3,1,0:T(8,128)}, u32[]{:S(2)}, u32[]{:S(2)}) %collective-permute-start.10) | collective-permute-done | bytes 1048608 | tf_op jit(solution)/shard_map/ppermute | solution.py:22
  168.6 1.3 multiply_add_fusion.14
  171.3 19.8 %collective-permute-done.2 = f32[2,2,128,512]{2,3,1,0:T(8,128)} collective-permute-done((f32[2,2,128,512]{2,3,1,0:T(8,128)}, f32[2,2,128,512]{2,3,1,0:T(8,128)}, u32[]{:S(2)}, u32[]{:S(2)}) %collective-permute-start.2) | collective-permute-done | bytes 1048608 | tf_op jit(solution)/shard_map/ppermute | solution.py:22
  191.1 1.3 multiply_add_fusion.22
  193.6 19.9 %collective-permute-done.11 = f32[2,2,128,512]{2,3,1,0:T(8,128)} collective-permute-done((f32[2,2,128,512]{2,3,1,0:T(8,128)}, f32[2,2,128,512]{2,3,1,0:T(8,128)}, u32[]{:S(2)}, u32[]{:S(2)}) %collective-permute-start.11) | collective-permute-done | bytes 1048608 | tf_op jit(solution)/shard_map/ppermute | solution.py:22
  213.5 1.3 multiply_add_fusion.13
  216.1 2.8 collective-permute-start.12
  219.1 16.9 %collective-permute-done.3 = f32[2,2,128,512]{2,3,1,0:T(8,128)} collective-permute-done((f32[2,2,128,512]{2,3,1,0:T(8,128)}, f32[2,2,128,512]{2,3,1,0:T(8,128)}, u32[]{:S(2)}, u32[]{:S(2)}) %collective-permute-start.3) | collective-permute-done | bytes 1048608 | tf_op jit(solution)/shard_map/ppermute | solution.py:22
  236.0 1.3 multiply_add_fusion.21
  238.5 2.8 collective-permute-start.4
  242.0 1.3 multiply_add_fusion.12
  246.0 18.6 %collective-permute-done.4 = f32[2,2,128,512]{2,3,1,0:T(8,128)} collective-permute-done((f32[2,2,128,512]{2,3,1,0:T(8,128)}, f32[2,2,128,512]{2,3,1,0:T(8,128)}, u32[]{:S(2)}, u32[]{:S(2)}) %collective-permute-start.4) | collective-permute-done | bytes 1048608 | tf_op jit(solution)/shard_map/ppermute | solution.py:22
  264.6 1.3 multiply_add_fusion.20
  268.4 18.8 %collective-permute-done.13 = f32[2,2,128,512]{2,3,1,0:T(8,128)} collective-permute-done((f32[2,2,128,512]{2,3,1,0:T(8,128)}, f32[2,2,128,512]{2,3,1,0:T(8,128)}, u32[]{:S(2)}, u32[]{:S(2)}) %collective-permute-start.13) | collective-permute-done | bytes 1048608 | tf_op jit(solution)/shard_map/ppermute | solution.py:22
  287.2 1.3 multiply_add_fusion.11
  289.8 2.9 collective-permute-start.14
  292.8 16.9 %collective-permute-done.5 = f32[2,2,128,512]{2,3,1,0:T(8,128)} collective-permute-done((f32[2,2,128,512]{2,3,1,0:T(8,128)}, f32[2,2,128,512]{2,3,1,0:T(8,128)}, u32[]{:S(2)}, u32[]{:S(2)}) %collective-permute-start.5) | collective-permute-done | bytes 1048608 | tf_op jit(solution)/shard_map/ppermute | solution.py:22
  309.7 1.3 multiply_add_fusion.19
  312.2 2.9 collective-permute-start.6
  315.1 1.3 multiply_add_fusion.10
  318.3 19.1 %collective-permute-done.6 = f32[2,2,128,512]{2,3,1,0:T(8,128)} collective-permute-done((f32[2,2,128,512]{2,3,1,0:T(8,128)}, f32[2,2,128,512]{2,3,1,0:T(8,128)}, u32[]{:S(2)}, u32[]{:S(2)}) %collective-permute-start.6) | collective-permute-done | bytes 1048608 | tf_op jit(solution)/shard_map/ppermute | solution.py:22
  337.4 1.3 multiply_add_fusion.18
  341.2 19.1 %collective-permute-done.15 = f32[2,2,128,512]{2,3,1,0:T(8,128)} collective-permute-done((f32[2,2,128,512]{2,3,1,0:T(8,128)}, f32[2,2,128,512]{2,3,1,0:T(8,128)}, u32[]{:S(2)}, u32[]{:S(2)}) %collective-permute-start.15) | collective-permute-done | bytes 1048608 | tf_op jit(solution)/shard_map/ppermute | solution.py:22
  360.3 1.3 multiply_add_fusion.9
  362.8 4.0 collective-permute-start.16
  366.8 16.0 %collective-permute-done.7 = f32[2,2,128,512]{2,3,1,0:T(8,128)} collective-permute-done((f32[2,2,128,512]{2,3,1,0:T(8,128)}, f32[2,2,128,512]{2,3,1,0:T(8,128)}, u32[]{:S(2)}, u32[]{:S(2)}) %collective-permute-start.7) | collective-permute-done | bytes 1048608 | tf_op jit(solution)/shard_map/ppermute | solution.py:22
  382.8 1.3 multiply_add_fusion.17
  384.3 2.5 collective-permute-start.8
  397.2 2.6 collective-permute-done.17
  400.2 1.4 collective-permute-start.18
  401.5 23.6 %collective-permute-done.18 = f32[2,2,128,512]{2,3,1,0:T(8,128)S(1)} collective-permute-done((f32[2,2,128,512]{2,3,1,0:T(8,128)S(1)}, f32[2,2,128,512]{2,3,1,0:T(8,128)S(1)}, u32[]{:S(2)}, u32[]{:S(2)}) %collective-permute-start.18) | collective-permute-done | bytes 1048608 | tf_op jit(solution)/shard_map/ppermute | solution.py:22
  425.4 1.6 collective-permute-start.19
  427.0 23.7 %collective-permute-done.19 = f32[2,2,128,512]{2,3,1,0:T(8,128)S(1)} collective-permute-done((f32[2,2,128,512]{2,3,1,0:T(8,128)S(1)}, f32[2,2,128,512]{2,3,1,0:T(8,128)S(1)}, u32[]{:S(2)}, u32[]{:S(2)}) %collective-permute-start.19) | collective-permute-done | bytes 1048608 | tf_op jit(solution)/shard_map/ppermute | solution.py:22
  452.2 21.7 %collective-permute-done.20 = f32[2,2,128,512]{2,3,1,0:T(8,128)S(1)} collective-permute-done((f32[2,2,128,512]{2,3,1,0:T(8,128)S(1)}, f32[2,2,128,512]{2,3,1,0:T(8,128)S(1)}, u32[]{:S(2)}, u32[]{:S(2)}) %collective-permute-start.20) | collective-permute-done | bytes 1048608 | tf_op jit(solution)/shard_map/ppermute | solution.py:22
  474.2 1.8 collective-permute-start.21
  476.0 21.7 %collective-permute-done.21 = f32[2,2,128,512]{2,3,1,0:T(8,128)S(1)} collective-permute-done((f32[2,2,128,512]{2,3,1,0:T(8,128)S(1)}, f32[2,2,128,512]{2,3,1,0:T(8,128)S(1)}, u32[]{:S(2)}, u32[]{:S(2)}) %collective-permute-start.21) | collective-permute-done | bytes 1048608 | tf_op jit(solution)/shard_map/ppermute | solution.py:22
  498.1 20.9 %collective-permute-done.22 = f32[2,2,128,512]{2,3,1,0:T(8,128)S(1)} collective-permute-done((f32[2,2,128,512]{2,3,1,0:T(8,128)S(1)}, f32[2,2,128,512]{2,3,1,0:T(8,128)S(1)}, u32[]{:S(2)}, u32[]{:S(2)}) %collective-permute-start.22) | collective-permute-done | bytes 1048608 | tf_op jit(solution)/shard_map/ppermute | solution.py:22
  519.3 5.2 collective-permute-start.23
  524.5 43.9 %collective-permute-done.23 = f32[2,2,128,512]{2,3,1,0:T(8,128)S(1)} collective-permute-done((f32[2,2,128,512]{2,3,1,0:T(8,128)S(1)}, f32[2,2,128,512]{2,3,1,0:T(8,128)S(1)}, u32[]{:S(2)}, u32[]{:S(2)}) %collective-permute-start.23) | collective-permute-done | bytes 1048608 | tf_op jit(solution)/shard_map/ppermute | solution.py:22
  569.6 48.9 %collective-permute-done.24 = f32[2,2,128,512]{2,3,1,0:T(8,128)S(1)} collective-permute-done((f32[2,2,128,512]{2,3,1,0:T(8,128)S(1)}, f32[2,2,128,512]{2,3,1,0:T(8,128)S(1)}, u32[]{:S(2)}, u32[]{:S(2)}) %collective-permute-start.24) | collective-permute-done | bytes 1048608 | tf_op jit(solution)/shard_map/ppermute | solution.py:22
  (111 shorter events, 44.9 us)
Async XLA Ops:
  1.2 8.0 %copy-start.1 = (bf16[3,128,512]{2,1,0:T(8,128)(2,1)S(1)}, bf16[3,128,512]{2,1,0:T(8,128)(2,1)}, u32[]{:S(2)}) copy-start(bf16[3,128,512]{2,1,0:T(8,128)(2,1)} %param.4) | copy-start | bytes 1179652
  1.3 13.0 %copy-start.2 = (f32[3,3,512]{2,1,0:T(4,128)S(1)}, f32[3,3,512]{2,1,0:T(4,128)}, u32[]{:S(2)}) copy-start(f32[3,3,512]{2,1,0:T(4,128)} %param.5) | copy-start | bytes 55300
  1.4 36.3 %collective-permute-start.9 = (f32[2,2,128,512]{2,3,1,0:T(8,128)S(1)}, f32[2,2,128,512]{2,3,1,0:T(8,128)}, u32[]{:S(2)}, u32[]{:S(2)}) collective-permute-start(f32[2,2,128,512]{2,3,1,0:T(8,128)S(1)} %pad_maximum_fusion.8), channel_id=1, source_target_pairs={{0,128},{128,0},{1,129},{129,1},{2,130},{130,2},{3,131},{131,3},{4... | collective-permute-start | bytes 3145736 | tf_op jit(solution)/shard_map/ppermute | solution.py:22
  10.3 9.1 %collective-permute-start = (bf16[3,2,512]{1,2,0:T(8,128)(2,1)}, bf16[3,2,512]{1,2,0:T(8,128)(2,1)S(1)}, u32[]{:S(2)}, u32[]{:S(2)}) collective-permute-start(bf16[3,2,512]{1,2,0:T(8,128)(2,1)} %copy.11), channel_id=1, source_target_pairs={{0,1},{1,2},{2,3},{3,4},{4,5},{5,6},{6,7},{7,8},{8,9},{9,10},{10,1... | collective-permute-start | bytes 18440 | tf_op jit(solution)/shard_map/ppermute | solution.py:12
  20.8 0.9 copy-start
  22.9 54.1 %collective-permute-start.1 = (f32[2,2,128,512]{2,3,1,0:T(8,128)}, f32[2,2,128,512]{2,3,1,0:T(8,128)}, u32[]{:S(2)}, u32[]{:S(2)}) collective-permute-start(f32[2,2,128,512]{2,3,1,0:T(8,128)} %pad_maximum_fusion), channel_id=1, source_target_pairs={{0,128},{128,0},{1,129},{129,1},{2,130},{130,2},{3,131},{131,3},{4... | collective-permute-start | bytes 3145736 | tf_op jit(solution)/shard_map/ppermute | solution.py:22
  40.2 128.4 %collective-permute-start.10 = (f32[2,2,128,512]{2,3,1,0:T(8,128)}, f32[2,2,128,512]{2,3,1,0:T(8,128)}, u32[]{:S(2)}, u32[]{:S(2)}) collective-permute-start(f32[2,2,128,512]{2,3,1,0:T(8,128)} %pad_maximum_fusion.9), channel_id=1, source_target_pairs={{0,64},{64,0},{1,65},{65,1},{2,66},{66,2},{3,67},{67,3},{4,68},{68... | collective-permute-start | bytes 3145736 | tf_op jit(solution)/shard_map/ppermute | solution.py:22
  79.5 111.6 %collective-permute-start.2 = (f32[2,2,128,512]{2,3,1,0:T(8,128)}, f32[2,2,128,512]{2,3,1,0:T(8,128)}, u32[]{:S(2)}, u32[]{:S(2)}) collective-permute-start(f32[2,2,128,512]{2,3,1,0:T(8,128)} %pad_maximum_fusion.1), channel_id=1, source_target_pairs={{0,64},{64,0},{1,65},{65,1},{2,66},{66,2},{3,67},{67,3},{4,68},{68... | collective-permute-start | bytes 3145736 | tf_op jit(solution)/shard_map/ppermute | solution.py:22
  171.1 42.4 %collective-permute-start.11 = (f32[2,2,128,512]{2,3,1,0:T(8,128)}, f32[2,2,128,512]{2,3,1,0:T(8,128)}, u32[]{:S(2)}, u32[]{:S(2)}) collective-permute-start(f32[2,2,128,512]{2,3,1,0:T(8,128)} %pad_maximum_fusion.10), channel_id=1, source_target_pairs={{0,32},{32,0},{1,33},{33,1},{2,34},{34,2},{3,35},{35,3},{4,36},{36... | collective-permute-start | bytes 3145736 | tf_op jit(solution)/shard_map/ppermute | solution.py:22
  193.6 42.4 %collective-permute-start.3 = (f32[2,2,128,512]{2,3,1,0:T(8,128)}, f32[2,2,128,512]{2,3,1,0:T(8,128)}, u32[]{:S(2)}, u32[]{:S(2)}) collective-permute-start(f32[2,2,128,512]{2,3,1,0:T(8,128)} %pad_maximum_fusion.2), channel_id=1, source_target_pairs={{0,32},{32,0},{1,33},{33,1},{2,34},{34,2},{3,35},{35,3},{4,36},{36... | collective-permute-start | bytes 3145736 | tf_op jit(solution)/shard_map/ppermute | solution.py:22
  216.1 25.9 %collective-permute-start.12 = (f32[2,2,128,512]{2,3,1,0:T(8,128)}, f32[2,2,128,512]{2,3,1,0:T(8,128)}, u32[]{:S(2)}, u32[]{:S(2)}) collective-permute-start(f32[2,2,128,512]{2,3,1,0:T(8,128)} %pad_maximum_fusion.11), channel_id=1, source_target_pairs={{0,16},{16,0},{1,17},{17,1},{2,18},{18,2},{3,19},{19,3},{4,20},{20... | collective-permute-start | bytes 3145736 | tf_op jit(solution)/shard_map/ppermute | solution.py:22
  238.5 26.1 %collective-permute-start.4 = (f32[2,2,128,512]{2,3,1,0:T(8,128)}, f32[2,2,128,512]{2,3,1,0:T(8,128)}, u32[]{:S(2)}, u32[]{:S(2)}) collective-permute-start(f32[2,2,128,512]{2,3,1,0:T(8,128)} %pad_maximum_fusion.3), channel_id=1, source_target_pairs={{0,16},{16,0},{1,17},{17,1},{2,18},{18,2},{3,19},{19,3},{4,20},{20... | collective-permute-start | bytes 3145736 | tf_op jit(solution)/shard_map/ppermute | solution.py:22
  244.5 42.7 %collective-permute-start.13 = (f32[2,2,128,512]{2,3,1,0:T(8,128)}, f32[2,2,128,512]{2,3,1,0:T(8,128)}, u32[]{:S(2)}, u32[]{:S(2)}) collective-permute-start(f32[2,2,128,512]{2,3,1,0:T(8,128)} %pad_maximum_fusion.12), channel_id=1, source_target_pairs={{0,8},{8,0},{1,9},{9,1},{2,10},{10,2},{3,11},{11,3},{4,12},{12,4},... | collective-permute-start | bytes 3145736 | tf_op jit(solution)/shard_map/ppermute | solution.py:22
  267.1 42.6 %collective-permute-start.5 = (f32[2,2,128,512]{2,3,1,0:T(8,128)}, f32[2,2,128,512]{2,3,1,0:T(8,128)}, u32[]{:S(2)}, u32[]{:S(2)}) collective-permute-start(f32[2,2,128,512]{2,3,1,0:T(8,128)} %pad_maximum_fusion.4), channel_id=1, source_target_pairs={{0,8},{8,0},{1,9},{9,1},{2,10},{10,2},{3,11},{11,3},{4,12},{12,4},... | collective-permute-start | bytes 3145736 | tf_op jit(solution)/shard_map/ppermute | solution.py:22
  289.8 25.4 %collective-permute-start.14 = (f32[2,2,128,512]{2,3,1,0:T(8,128)}, f32[2,2,128,512]{2,3,1,0:T(8,128)}, u32[]{:S(2)}, u32[]{:S(2)}) collective-permute-start(f32[2,2,128,512]{2,3,1,0:T(8,128)} %pad_maximum_fusion.13), channel_id=1, source_target_pairs={{0,4},{4,0},{1,5},{5,1},{2,6},{6,2},{3,7},{7,3},{8,12},{12,8},{9,1... | collective-permute-start | bytes 3145736 | tf_op jit(solution)/shard_map/ppermute | solution.py:22
  312.2 25.2 %collective-permute-start.6 = (f32[2,2,128,512]{2,3,1,0:T(8,128)}, f32[2,2,128,512]{2,3,1,0:T(8,128)}, u32[]{:S(2)}, u32[]{:S(2)}) collective-permute-start(f32[2,2,128,512]{2,3,1,0:T(8,128)} %pad_maximum_fusion.5), channel_id=1, source_target_pairs={{0,4},{4,0},{1,5},{5,1},{2,6},{6,2},{3,7},{7,3},{8,12},{12,8},{9,1... | collective-permute-start | bytes 3145736 | tf_op jit(solution)/shard_map/ppermute | solution.py:22
  317.7 42.6 %collective-permute-start.15 = (f32[2,2,128,512]{2,3,1,0:T(8,128)}, f32[2,2,128,512]{2,3,1,0:T(8,128)}, u32[]{:S(2)}, u32[]{:S(2)}) collective-permute-start(f32[2,2,128,512]{2,3,1,0:T(8,128)} %pad_maximum_fusion.14), channel_id=1, source_target_pairs={{0,2},{2,0},{1,3},{3,1},{4,6},{6,4},{5,7},{7,5},{8,10},{10,8},{9,1... | collective-permute-start | bytes 3145736 | tf_op jit(solution)/shard_map/ppermute | solution.py:22
  339.9 42.9 %collective-permute-start.7 = (f32[2,2,128,512]{2,3,1,0:T(8,128)}, f32[2,2,128,512]{2,3,1,0:T(8,128)}, u32[]{:S(2)}, u32[]{:S(2)}) collective-permute-start(f32[2,2,128,512]{2,3,1,0:T(8,128)} %pad_maximum_fusion.6), channel_id=1, source_target_pairs={{0,2},{2,0},{1,3},{3,1},{4,6},{6,4},{5,7},{7,5},{8,10},{10,8},{9,1... | collective-permute-start | bytes 3145736 | tf_op jit(solution)/shard_map/ppermute | solution.py:22
  362.8 24.0 %collective-permute-start.16 = (f32[2,2,128,512]{2,3,1,0:T(8,128)}, f32[2,2,128,512]{2,3,1,0:T(8,128)S(1)}, u32[]{:S(2)}, u32[]{:S(2)}) collective-permute-start(f32[2,2,128,512]{2,3,1,0:T(8,128)} %pad_maximum_fusion.15), channel_id=1, source_target_pairs={{0,1},{1,0},{2,3},{3,2},{4,5},{5,4},{6,7},{7,6},{8,9},{9,8},{10,11... | collective-permute-start | bytes 3145736 | tf_op jit(solution)/shard_map/ppermute | solution.py:22
  384.3 5.9 collective-permute-start.8
  397.1 2.7 collective-permute-start.17
  400.2 25.0 %collective-permute-start.18 = (f32[2,2,128,512]{2,3,1,0:T(8,128)S(1)}, f32[2,2,128,512]{2,3,1,0:T(8,128)S(1)}, u32[]{:S(2)}, u32[]{:S(2)}) collective-permute-start(f32[2,2,128,512]{2,3,1,0:T(8,128)S(1)} %pad_maximum_fusion.17), channel_id=1, source_target_pairs={{0,2},{2,0},{1,3},{3,1},{4,6},{6,4},{5,7},{7,5},{8,10},{10,8},{9,1... | collective-permute-start | bytes 3145736 | tf_op jit(solution)/shard_map/ppermute | solution.py:22
  425.4 25.3 %collective-permute-start.19 = (f32[2,2,128,512]{2,3,1,0:T(8,128)S(1)}, f32[2,2,128,512]{2,3,1,0:T(8,128)S(1)}, u32[]{:S(2)}, u32[]{:S(2)}) collective-permute-start(f32[2,2,128,512]{2,3,1,0:T(8,128)S(1)} %pad_maximum_fusion.18), channel_id=1, source_target_pairs={{0,4},{4,0},{1,5},{5,1},{2,6},{6,2},{3,7},{7,3},{8,12},{12,8},{9,1... | collective-permute-start | bytes 3145736 | tf_op jit(solution)/shard_map/ppermute | solution.py:22
  451.0 22.9 %collective-permute-start.20 = (f32[2,2,128,512]{2,3,1,0:T(8,128)S(1)}, f32[2,2,128,512]{2,3,1,0:T(8,128)S(1)}, u32[]{:S(2)}, u32[]{:S(2)}) collective-permute-start(f32[2,2,128,512]{2,3,1,0:T(8,128)S(1)} %pad_maximum_fusion.19), channel_id=1, source_target_pairs={{0,8},{8,0},{1,9},{9,1},{2,10},{10,2},{3,11},{11,3},{4,12},{12,4},... | collective-permute-start | bytes 3145736 | tf_op jit(solution)/shard_map/ppermute | solution.py:22
  474.2 23.5 %collective-permute-start.21 = (f32[2,2,128,512]{2,3,1,0:T(8,128)S(1)}, f32[2,2,128,512]{2,3,1,0:T(8,128)S(1)}, u32[]{:S(2)}, u32[]{:S(2)}) collective-permute-start(f32[2,2,128,512]{2,3,1,0:T(8,128)S(1)} %pad_maximum_fusion.20), channel_id=1, source_target_pairs={{0,16},{16,0},{1,17},{17,1},{2,18},{18,2},{3,19},{19,3},{4,20},{20... | collective-permute-start | bytes 3145736 | tf_op jit(solution)/shard_map/ppermute | solution.py:22
  498.0 21.0 %collective-permute-start.22 = (f32[2,2,128,512]{2,3,1,0:T(8,128)S(1)}, f32[2,2,128,512]{2,3,1,0:T(8,128)S(1)}, u32[]{:S(2)}, u32[]{:S(2)}) collective-permute-start(f32[2,2,128,512]{2,3,1,0:T(8,128)S(1)} %pad_maximum_fusion.21), channel_id=1, source_target_pairs={{0,32},{32,0},{1,33},{33,1},{2,34},{34,2},{3,35},{35,3},{4,36},{36... | collective-permute-start | bytes 3145736 | tf_op jit(solution)/shard_map/ppermute | solution.py:22
  519.3 49.1 %collective-permute-start.23 = (f32[2,2,128,512]{2,3,1,0:T(8,128)S(1)}, f32[2,2,128,512]{2,3,1,0:T(8,128)S(1)}, u32[]{:S(2)}, u32[]{:S(2)}) collective-permute-start(f32[2,2,128,512]{2,3,1,0:T(8,128)S(1)} %pad_maximum_fusion.22), channel_id=1, source_target_pairs={{0,64},{64,0},{1,65},{65,1},{2,66},{66,2},{3,67},{67,3},{4,68},{68... | collective-permute-start | bytes 3145736 | tf_op jit(solution)/shard_map/ppermute | solution.py:22
  568.7 49.8 %copy-start.3 = (f32[512]{0:T(512)S(1)}, f32[512]{0:T(512)}, u32[]{:S(2)}) copy-start(f32[512]{0:T(512)} %param.7) | copy-start | bytes 6148
  568.7 49.7 %collective-permute-start.24 = (f32[2,2,128,512]{2,3,1,0:T(8,128)S(1)}, f32[2,2,128,512]{2,3,1,0:T(8,128)S(1)}, u32[]{:S(2)}, u32[]{:S(2)}) collective-permute-start(f32[2,2,128,512]{2,3,1,0:T(8,128)S(1)} %pad_maximum_fusion.23), channel_id=1, source_target_pairs={{0,128},{128,0},{1,129},{129,1},{2,130},{130,2},{3,131},{131,3},{4... | collective-permute-start | bytes 3145736 | tf_op jit(solution)/shard_map/ppermute | solution.py:22
where the time goes:
time: 622 us; the launch traced here: 620 us
  waiting for transfers between devices  485 us (78%)
  starting transfers between devices  79.3 us (13%)
  other arithmetic  40.6 us (7%)
  matrix products  9.89 us (2%)
    ppermute x24, waiting for transfers between devices, from_partner(): return lax.ppermute(block, axis, route)  480 us
    ppermute x24, starting transfers between devices, from_partner(): return lax.ppermute(block, axis, route)  75.3 us
    add x16, other arithmetic, forward_step(): factors[0] * current + received  18.8 us
    another operation x22, other arithmetic, complex_scale(): jnp.stack([paired[0] * scale_re - paired[1] * scale_im, paired[0] * scale...  14.5 us
  transfers between devices with their start and end apart: 25, of which 22 were waited for; matrix products, arithmetic and copies ran while one was open for 7% of the time, Pallas kernels for 0%

commit v1 on v0

v1 whole, which is shorter than its diff:
```python
import functools
import math

import jax
import jax.numpy as jnp
import ml_dtypes
import numpy as np
from jax import lax
from jax.experimental import pallas as pl
from jax.experimental.pallas import tpu as pltpu
from jax.sharding import PartitionSpec as P

MESH = pl.DeviceIdType.MESH
F32, BF16 = jnp.float32, jnp.bfloat16

DEPTH = 8
ROWS = 128
LANES = 128
PAIR = 2


def halves(table):
    high = table.astype(np.float32).astype(ml_dtypes.bfloat16)
    low = (table - high.astype(np.float64)).astype(ml_dtypes.bfloat16)
    return np.stack([high, low])


def tables(count):
    total = count * ROWS
    segment = np.arange(count)
    phase = 2 * np.pi * ((4 * segment[:, None] + 1) * segment[None, :] % (4 * count)) / (4 * count)
    outer = np.concatenate([np.cos(phase), -np.sin(phase)])
    inner_index = np.arange(ROWS)
    angle = 2 * np.pi * (inner_index[:, None] * inner_index[None, :] % ROWS) / ROWS
    cos, sin = np.cos(angle), np.sin(angle)
    inner = np.block([[cos, -sin], [sin, cos]])
    inner_back = np.block([[cos, sin], [-sin, cos]])
    turn = 2 * np.pi * ((4 * segment[:, None] + 1) * inner_index[None, :]) / (4 * total)
    twiddle = np.stack([np.cos(turn), -np.sin(turn)]).astype(np.float32)
    return halves(outer), halves(outer.T / total), halves(inner), halves(inner_back), twiddle


def split(value):
    high = value.astype(BF16)
    return high, (value - high.astype(F32)).astype(BF16)


def dot(a, b):
    return jnp.dot(a, b, preferred_element_type=F32)


def table_times(table, value):
    high, low = split(value)
    return dot(table[0], high) + (dot(table[0], low) + dot(table[1], high))


def times_table(value, table):
    high, low = split(value)
    return dot(high, table[0]) + (dot(high, table[1]) + dot(low, table[0]))


def spectrum(signal, outer, inner, twiddle):
    count = signal.shape[0]
    stage = table_times(outer, signal)
    parts = []
    for channel in range(PAIR):
        lanes = slice(channel * LANES, (channel + 1) * LANES)
        re, im = stage[:count, lanes], stage[count:, lanes]
        parts.append(
            jnp.concatenate([re * twiddle[0] - im * twiddle[1], re * twiddle[1] + im * twiddle[0]], axis=1)
        )
    return times_table(jnp.concatenate(parts, axis=0), inner)


def signal_of(product, outer_back, inner_back, twiddle):
    count = product.shape[0] // PAIR
    stage = times_table(product, inner_back)
    reals, imags = [], []
    for channel in range(PAIR):
        re = stage[channel * count : (channel + 1) * count, :LANES]
        im = stage[channel * count : (channel + 1) * count, LANES:]
        reals.append(re * twiddle[0] + im * twiddle[1])
        imags.append(im * twiddle[0] - re * twiddle[1])
    both = jnp.concatenate([jnp.concatenate(reals, axis=1), jnp.concatenate(imags, axis=1)], axis=0)
    return table_times(outer_back, both)


def kernel(
    count,
    projected,
    taps,
    long_filter,
    skip,
    outer_hbm,
    outer_back_hbm,
    inner_hbm,
    inner_back_hbm,
    twiddle_hbm,
    gated,
    streams,
    filt,
    outer,
    outer_back,
    inner,
    inner_back,
    twiddle,
    rim_out,
    rim_in,
    turned,
    h_out,
    h_z,
    h_mid,
    h_in,
    x_out,
    x_p,
    x_mid,
    x_in,
    y_out,
    y_z,
    y_mid,
    y_in,
    mixed,
    query,
    spec_h,
    load_sem,
    send_sem,
    recv_sem,
):
    me = lax.axis_index("ctx")
    plane = count // DEPTH
    z = me // plane
    p = me % plane
    right = (me + 1) % count
    left = (me + count - 1) % count

    def plane_peer(step):
        q = (p + step) % plane
        return q, z * plane + q

    def z_peer(step):
        q = (z + step) % DEPTH
        return q, q * plane + p

    loads = [
        pltpu.make_async_copy(src, dst, load_sem.at[i])
        for i, (src, dst) in enumerate(
            [
                (long_filter, filt),
                (projected, streams),
                (outer_hbm, outer),
                (inner_hbm, inner),
                (twiddle_hbm, twiddle),
                (inner_back_hbm, inner_back),
                (outer_back_hbm, outer_back),
            ]
        )
    ]
    for load in loads:
        load.start()

    barrier = pltpu.get_barrier_semaphore()

    def signal(device):
        pl.semaphore_signal(barrier, inc=1, device_id=(device,), device_id_type=MESH)

    @pl.loop(1, plane)
    def _(step):
        signal(plane_peer(step)[1])

    @pl.loop(1, DEPTH)
    def _(step):
        signal(z_peer(step)[1])

    signal(right)
    signal(left)

    def rows(index, size):
        return pl.ds(pl.multiple_of(index * size, size), size)

    def send(phase, src, dst, device):
        pltpu.make_async_remote_copy(
            src_ref=src,
            dst_ref=dst,
            send_sem=send_sem.at[phase],
            recv_sem=recv_sem.at[phase],
            device_id=(device,),
            device_id_type=MESH,
        ).start()

    def arrived(phase, src, dst, size):
        done = pltpu.make_async_remote_copy(
            src_ref=src.at[pl.ds(0, size)],
            dst_ref=dst.at[pl.ds(0, size)],
            send_sem=send_sem.at[phase],
            recv_sem=recv_sem.at[phase],
            device_id=(right,),
            device_id_type=MESH,
        )
        done.wait_send()
        done.wait_recv()

    def over_plane(phase, src, dst):
        size = 2 * DEPTH

        @pl.loop(1, plane)
        def _(step):
            q, device = plane_peer(step)
            send(phase, src.at[rows(q, size)], dst.at[rows(p, size)], device)

        dst[rows(p, size), :] = src[rows(p, size), :]

    def over_z(phase, src, dst):
        size = 2 * plane

        @pl.loop(1, DEPTH)
        def _(step):
            q, device = z_peer(step)
            send(phase, src.at[rows(q, size)], dst.at[rows(z, size)], device)

        dst[rows(z, size), :] = src[rows(z, size), :]

    plane_rows = 2 * DEPTH * (plane - 1)
    z_rows = 2 * plane * (DEPTH - 1)

    def by_z(src, dst):
        for index in range(2 * DEPTH):
            dst[pl.ds(index * plane, plane), :] = src[pl.ds(index, plane, 2 * DEPTH), :]

    loads[0].wait()
    for block in range(4):
        lanes = pl.ds(block * LANES, LANES)
        turned[lanes, :] = filt[:, lanes].T
    by_z(turned, h_out)

    loads[1].wait()
    for stream in range(3):
        tail = streams[stream, ROWS - 16 : ROWS, :].astype(F32)
        rim_out[2 * stream : 2 * stream + 2, :] = tail[14:16, :]
    rim_out[6:8, :] = jnp.zeros_like(rim_out[6:8, :])

    pl.semaphore_wait(barrier, plane - 1 + DEPTH - 1 + 2)
    send(0, rim_out, rim_in, right)
    over_z(1, h_out, h_z)
    arrived(0, rim_out, rim_in, 8)

    row = lax.broadcasted_iota(jnp.int32, (ROWS, 1), 0)
    first = me == 0

    def short(stream):
        here = streams[stream].astype(F32)
        rim = jnp.where(first, 0.0, rim_in[2 * stream : 2 * stream + 2, :])
        one = jnp.where(row == 0, rim[1:2, :], pltpu.roll(here, 1, 0))
        two = jnp.where(row == 0, rim[0:1, :], jnp.where(row == 1, rim[1:2, :], pltpu.roll(here, 2, 0)))
        return (
            taps[stream, 0:1, :] * here + taps[stream, 1:2, :] * one + taps[stream, 2:3, :] * two
        )

    mixed[...] = short(1) * short(2)
    for block in range(4):
        lanes = pl.ds(block * LANES, LANES)
        x_out[lanes, :] = mixed[:, lanes].T
    over_plane(2, x_out, x_p)

    arrived(1, h_out, h_z, z_rows)
    for q in range(plane):
        for channel in range(PAIR):
            h_mid[pl.ds(q * 2 * DEPTH + channel * DEPTH, DEPTH), :] = h_z[
                pl.ds(channel * plane + q, DEPTH, 2 * plane), :
            ]
    arrived(2, x_out, x_p, plane_rows)
    by_z(x_p, x_mid)
    over_z(4, x_mid, x_in)
    over_plane(3, h_mid, h_in)

    query[...] = short(0)
    mixed[...] = skip[...] * mixed[...]
    for load in loads[2:]:
        load.wait()

    arrived(3, h_mid, h_in, plane_rows)
    channels = []
    for channel in range(PAIR):
        channels.append(
            jnp.concatenate(
                [h_in[pl.ds(channel * DEPTH + s, plane, 2 * DEPTH), :] for s in range(DEPTH)], axis=0
            )
        )
    spec_h[...] = spectrum(jnp.concatenate(channels, axis=1), outer, inner, twiddle)

    arrived(4, x_mid, x_in, z_rows)
    channels = []
    for channel in range(PAIR):
        channels.append(
            jnp.concatenate(
                [x_in[pl.ds((2 * s + channel) * plane, plane), :] for s in range(DEPTH)], axis=0
            )
        )
    spec_x = spectrum(jnp.concatenate(channels, axis=1), outer, inner, twiddle)
    xr, xi = spec_x[:, :LANES], spec_x[:, LANES:]
    hr, hi = spec_h[:, :LANES], spec_h[:, LANES:]
    product = jnp.concatenate([xr * hr - xi * hi, xr * hi + xi * hr], axis=1)
    result = signal_of(product, outer_back, inner_back, twiddle)
    for s in range(DEPTH):
        for channel in range(PAIR):
            y_out[pl.ds((2 * s + channel) * plane, plane), :] = result[
                s * plane : (s + 1) * plane, channel * LANES : (channel + 1) * LANES
            ]
    over_z(5, y_out, y_z)
    arrived(5, y_out, y_z, z_rows)
    for q in range(plane):
        y_mid[pl.ds(q * 2 * DEPTH, 2 * DEPTH), :] = y_z[pl.ds(q, 2 * DEPTH, plane), :]
    over_plane(6, y_mid, y_in)
    arrived(6, y_mid, y_in, plane_rows)
    for block in range(4):
        lanes = pl.ds(block * LANES, LANES)
        convolved = y_in[lanes, :].T
        gated[:, lanes] = (query[:, lanes] * (convolved + mixed[:, lanes])).astype(BF16)


def per_device(count, consts, projected, short_taps, long_filter, skip_weight):
    channels = long_filter.shape[1]
    outer, outer_back, inner, inner_back, twiddle = consts
    block = pltpu.VMEM((channels, LANES), F32)
    wide = pltpu.VMEM((ROWS, channels), F32)
    vmem = pl.BlockSpec(memory_space=pltpu.VMEM)
    anywhere = pl.BlockSpec(memory_space=pl.ANY)
    return pl.pallas_call(
        functools.partial(kernel, count),
        out_shape=jax.ShapeDtypeStruct((ROWS, channels), BF16),
        in_specs=[anywhere, vmem, anywhere, vmem] + [anywhere] * 5,
        out_specs=vmem,
        scratch_shapes=[
            pltpu.VMEM(projected.shape, BF16),
            wide,
            *[pltpu.VMEM(c.shape, c.dtype) for c in consts],
            pltpu.VMEM((8, channels), F32),
            pltpu.VMEM((8, channels), F32),
            *[block] * 13,
            wide,
            wide,
            pltpu.VMEM((PAIR * count, 2 * LANES), F32),
            pltpu.SemaphoreType.DMA((7,)),
            pltpu.SemaphoreType.DMA((7,)),
            pltpu.SemaphoreType.DMA((7,)),
        ],
        compiler_params=pltpu.CompilerParams(
            collective_id=0, has_side_effects=True, vmem_limit_bytes=60 * 1024 * 1024
        ),
    )(projected, short_taps, long_filter, skip_weight.reshape(1, channels), *consts)


def solution(mesh):
    count = mesh.shape["ctx"]
    consts = [jnp.asarray(t) for t in tables(count)]
    return jax.shard_map(
        functools.partial(per_device, count, consts),
        mesh=mesh,
        in_specs=(P(None, "ctx", None), P(), P("ctx", None), P()),
        out_specs=P("ctx", None),
        check_vma=False,
    )
```

time: 622 us -> 50 us (0.08)
  waiting for transfers between devices: 485 us -> 0 us
  starting transfers between devices: 79.3 us -> 0 us
  Pallas kernels: 0 us -> 48.3 us
  other arithmetic: 40.6 us -> 0 us
  matrix products: 9.89 us -> 0 us
    ppermute x25 -> x0, waiting for transfers between devices: 485 us -> none  [the longest x24 480 us: from_partner(): return lax.ppermute(block, axis, route)]
    ppermute x25 -> x0, starting transfers between devices: 79.3 us -> none  [the longest x24 75.3 us: from_partner(): return lax.ppermute(block, axis, route)]
    pallas_call x0 -> x1, Pallas kernels: none -> 48.3 us  [per_device(): pl.pallas_call(functools.partial(kernel, count), out_shape=jax.ShapeDtype...]
    add x26 -> x0, other arithmetic: 20.9 us -> none  [the longest x16 18.8 us: forward_step(): factors[0] * current + received]
    another operation x27 -> x0, other arithmetic: 15.8 us -> none  [the longest x22 14.5 us: complex_scale(): jnp.stack([paired[0] * scale_re - paired[1] * scale_im, paired[0] * scale...]
    dot_general x12 -> x0, matrix products: 9.89 us -> none  [the longest x8 6.59 us: apply_forward(): jnp.einsum('rk,src->skc', matrix, part, precision=lax.Precision.HIGHEST)]
  transfers between devices with their start and end apart: 25 -> 0, of which waited for: 22 -> 0; matrix products, arithmetic and copies ran while one was open for 7% -> 0% of each run, Pallas kernels for 0% -> 0%
where the time goes in v1:
time: 50 us; the launch traced here: 49.8 us
  Pallas kernels  48.3 us (97%)
  local copies, waits for them, and re-layouts  1.57 us (3%)
    pallas_call x1, Pallas kernels, per_device(): pl.pallas_call(functools.partial(kernel, count), out_shape=jax.ShapeDtype...  48.3 us
    unnamed x1, local copies, waits for them, and re-layouts  1.57 us

profile of v1, /device:TPU:1, one launch (start us, length us, event | category | flops | bytes accessed | tf_op | source)
XLA Modules:
  0.0 49.8 jit_solution(7044027495995193724)
XLA Ops:
  0.0 48.3 %shard_map.91 = bf16[128,512]{1,0:T(8,128)(2,1)} custom-call(bf16[3,128,512]{2,1,0:T(8,128)(2,1)} %projected.1, f32[3,3,512]{2,1,0:T(4,128)} %taps.1, f32[128,512]{1,0:T(8,128)} %long_filter.1, f32[1,512]{1,0:T(1,128)} %bitcast.1, bf16[2,512,256]{2,1,0:T(8,128)(2,1)} %constant.10.clone.outer_hbm, bf16[2,256,512]{2,1,0:T(8,128)(2,1)} %constant.11.clone.outer_back_hbm, ...), custom_call_target="tpu_custom_call" | custom-call | tf_op jit(solution)/shard_map/pallas_call | solution.py:327
  48.3 1.6 %copy.11 = bf16[128,512]{1,0:T(8,128)(2,1)} copy(bf16[128,512]{1,0:T(8,128)(2,1)} %shard_map.91) | data formatting | bytes 262144

commit v2 on v1

--- a/solution.py
+++ b/solution.py
@@ -17,6 +17,9 @@
 ROWS = 128
 LANES = 128
 PAIR = 2
+GROUP = 8
+BATCH = 15
+STRIDE = 37
 
 
 def halves(table):
@@ -106,18 +109,13 @@
     twiddle,
     rim_out,
     rim_in,
-    turned,
     h_out,
     h_z,
     h_mid,
     h_in,
     x_out,
-    x_p,
-    x_mid,
     x_in,
     y_out,
-    y_z,
-    y_mid,
     y_in,
     mixed,
     query,
@@ -125,21 +123,15 @@
     load_sem,
     send_sem,
     recv_sem,
+    ready,
 ):
     me = lax.axis_index("ctx")
     plane = count // DEPTH
     z = me // plane
     p = me % plane
+    unit = me % GROUP
     right = (me + 1) % count
     left = (me + count - 1) % count
-
-    def plane_peer(step):
-        q = (p + step) % plane
-        return q, z * plane + q
-
-    def z_peer(step):
-        q = (z + step) % DEPTH
-        return q, q * plane + p
 
     loads = [
         pltpu.make_async_copy(src, dst, load_sem.at[i])
@@ -155,82 +147,65 @@
             ]
         )
     ]
-    for load in loads:
+    loads[0].start()
+
+    barrier = pltpu.get_barrier_semaphore()
+
+    def signal(semaphore, device):
+        pl.semaphore_signal(semaphore, inc=1, device_id=(device,), device_id_type=MESH)
+
+    def over_group(semaphore):
+        for step in range(1, GROUP):
+            signal(semaphore, me - unit + lax.rem(unit + step, GROUP))
+
+    def over_plane(semaphore):
+        for step in range(1, plane // GROUP):
+            signal(semaphore, z * plane + lax.rem(p + step * GROUP, plane))
+
+    def over_z(semaphore):
+        for step in range(1, DEPTH):
+            signal(semaphore, lax.rem(me + step * plane, count))
+
+    over_z(barrier)
+    signal(barrier, right)
+    signal(barrier, left)
+    over_plane(barrier)
+    over_group(barrier)
+    for load in loads[1:]:
         load.start()
 
-    barrier = pltpu.get_barrier_semaphore()
-
-    def signal(device):
-        pl.semaphore_signal(barrier, inc=1, device_id=(device,), device_id_type=MESH)
-
-    @pl.loop(1, plane)
-    def _(step):
-        signal(plane_peer(step)[1])
-
-    @pl.loop(1, DEPTH)
-    def _(step):
-        signal(z_peer(step)[1])
-
-    signal(right)
-    signal(left)
-
-    def rows(index, size):
-        return pl.ds(pl.multiple_of(index * size, size), size)
-
-    def send(phase, src, dst, device):
-        pltpu.make_async_remote_copy(
+    def copy(phase, src, dst, device):
+        return pltpu.make_async_remote_copy(
             src_ref=src,
             dst_ref=dst,
             send_sem=send_sem.at[phase],
             recv_sem=recv_sem.at[phase],
             device_id=(device,),
             device_id_type=MESH,
-        ).start()
-
-    def arrived(phase, src, dst, size):
-        done = pltpu.make_async_remote_copy(
-            src_ref=src.at[pl.ds(0, size)],
-            dst_ref=dst.at[pl.ds(0, size)],
-            send_sem=send_sem.at[phase],
-            recv_sem=recv_sem.at[phase],
-            device_id=(right,),
-            device_id_type=MESH,
         )
+
+    def own_rows(device):
+        return pl.ds(pl.multiple_of(device * PAIR, PAIR), PAIR)
+
+    def exchange(phase, src, dst):
+        @pl.loop(0, (count - 1) // BATCH)
+        def _(batch):
+            for step in range(1, BATCH + 1):
+                device = lax.rem(me + (batch * BATCH + step) * STRIDE, count)
+                copy(phase, src.at[own_rows(device)], dst.at[own_rows(me)], device).start()
+
+        dst[own_rows(me), :] = src[own_rows(me), :]
+
+    def arrived(phase, src, dst, own):
+        rows = pl.ds(0, PAIR * count - own)
+        done = copy(phase, src.at[rows], dst.at[rows], right)
         done.wait_send()
         done.wait_recv()
-
-    def over_plane(phase, src, dst):
-        size = 2 * DEPTH
-
-        @pl.loop(1, plane)
-        def _(step):
-            q, device = plane_peer(step)
-            send(phase, src.at[rows(q, size)], dst.at[rows(p, size)], device)
-
-        dst[rows(p, size), :] = src[rows(p, size), :]
-
-    def over_z(phase, src, dst):
-        size = 2 * plane
-
-        @pl.loop(1, DEPTH)
-        def _(step):
-            q, device = z_peer(step)
-            send(phase, src.at[rows(q, size)], dst.at[rows(z, size)], device)
-
-        dst[rows(z, size), :] = src[rows(z, size), :]
-
-    plane_rows = 2 * DEPTH * (plane - 1)
-    z_rows = 2 * plane * (DEPTH - 1)
-
-    def by_z(src, dst):
-        for index in range(2 * DEPTH):
-            dst[pl.ds(index * plane, plane), :] = src[pl.ds(index, plane, 2 * DEPTH), :]
 
     loads[0].wait()
     for block in range(4):
         lanes = pl.ds(block * LANES, LANES)
-        turned[lanes, :] = filt[:, lanes].T
-    by_z(turned, h_out)
+        h_out[lanes, :] = filt[:, lanes].T
 
     loads[1].wait()
     for stream in range(3):
@@ -238,10 +213,23 @@
         rim_out[2 * stream : 2 * stream + 2, :] = tail[14:16, :]
     rim_out[6:8, :] = jnp.zeros_like(rim_out[6:8, :])
 
-    pl.semaphore_wait(barrier, plane - 1 + DEPTH - 1 + 2)
-    send(0, rim_out, rim_in, right)
-    over_z(1, h_out, h_z)
-    arrived(0, rim_out, rim_in, 8)
+    pl.semaphore_wait(barrier, GROUP - 1 + plane // GROUP - 1 + DEPTH - 1 + 2)
+    over_plane(ready.at[0])
+    rim = copy(0, rim_out, rim_in, right)
+    rim.start()
+    column = PAIR * plane
+
+    def piece(index, size):
+        return pl.ds(pl.multiple_of(index * size, size), size)
+
+    for step in range(1, DEPTH):
+        other = lax.rem(z + step, DEPTH)
+        copy(1, h_out.at[piece(other, column)], h_z.at[piece(z, column)], other * plane + p).start()
+    h_z[piece(z, column), :] = h_out[piece(z, column), :]
+
+    pl.semaphore_wait(ready.at[0], plane // GROUP - 1)
+    over_z(ready.at[1])
+    rim.wait()
 
     row = lax.broadcasted_iota(jnp.int32, (ROWS, 1), 0)
     first = me == 0
@@ -259,58 +247,45 @@
     for block in range(4):
         lanes = pl.ds(block * LANES, LANES)
         x_out[lanes, :] = mixed[:, lanes].T
-    over_plane(2, x_out, x_p)
-
-    arrived(1, h_out, h_z, z_rows)
-    for q in range(plane):
-        for channel in range(PAIR):
-            h_mid[pl.ds(q * 2 * DEPTH + channel * DEPTH, DEPTH), :] = h_z[
-                pl.ds(channel * plane + q, DEPTH, 2 * plane), :
-            ]
-    arrived(2, x_out, x_p, plane_rows)
-    by_z(x_p, x_mid)
-    over_z(4, x_mid, x_in)
-    over_plane(3, h_mid, h_in)
+    pl.semaphore_wait(ready.at[1], DEPTH - 1)
+    exchange(2, x_out, x_in)
+
+    arrived(1, h_out, h_z, column)
+    part = PAIR * DEPTH
+    for other in range(plane):
+        for c in range(PAIR):
+            h_mid[pl.ds(other * part + c * DEPTH, DEPTH), :] = h_z[pl.ds(PAIR * other + c, DEPTH, column), :]
+
+    @pl.loop(1, plane)
+    def _(step):
+        other = lax.rem(p + step, plane)
+        copy(4, h_mid.at[piece(other, part)], h_in.at[piece(p, part)], z * plane + other).start()
+
+    h_in[piece(p, part), :] = h_mid[piece(p, part), :]
 
     query[...] = short(0)
     mixed[...] = skip[...] * mixed[...]
     for load in loads[2:]:
         load.wait()
 
-    arrived(3, h_mid, h_in, plane_rows)
-    channels = []
-    for channel in range(PAIR):
-        channels.append(
-            jnp.concatenate(
-                [h_in[pl.ds(channel * DEPTH + s, plane, 2 * DEPTH), :] for s in range(DEPTH)], axis=0
-            )
-        )
-    spec_h[...] = spectrum(jnp.concatenate(channels, axis=1), outer, inner, twiddle)
-
-    arrived(4, x_mid, x_in, z_rows)
-    channels = []
-    for channel in range(PAIR):
-        channels.append(
-            jnp.concatenate(
-                [x_in[pl.ds((2 * s + channel) * plane, plane), :] for s in range(DEPTH)], axis=0
-            )
-        )
-    spec_x = spectrum(jnp.concatenate(channels, axis=1), outer, inner, twiddle)
+    arrived(4, h_mid, h_in, part)
+    filters = [
+        jnp.concatenate([h_in[pl.ds(c * DEPTH + s, plane, part), :] for s in range(DEPTH)], axis=0)
+        for c in range(PAIR)
+    ]
+    spec_h[...] = spectrum(jnp.concatenate(filters, axis=1), outer, inner, twiddle)
+
+    arrived(2, x_out, x_in, PAIR)
+    signals = [x_in[pl.ds(c, count, PAIR), :] for c in range(PAIR)]
+    spec_x = spectrum(jnp.concatenate(signals, axis=1), outer, inner, twiddle)
     xr, xi = spec_x[:, :LANES], spec_x[:, LANES:]
     hr, hi = spec_h[:, :LANES], spec_h[:, LANES:]
     product = jnp.concatenate([xr * hr - xi * hi, xr * hi + xi * hr], axis=1)
     result = signal_of(product, outer_back, inner_back, twiddle)
-    for s in range(DEPTH):
-        for channel in range(PAIR):
-            y_out[pl.ds((2 * s + channel) * plane, plane), :] = result[
-                s * plane : (s + 1) * plane, channel * LANES : (channel + 1) * LANES
-            ]
-    over_z(5, y_out, y_z)
-    arrived(5, y_out, y_z, z_rows)
-    for q in range(plane):
-        y_mid[pl.ds(q * 2 * DEPTH, 2 * DEPTH), :] = y_z[pl.ds(q, 2 * DEPTH, plane), :]
-    over_plane(6, y_mid, y_in)
-    arrived(6, y_mid, y_in, plane_rows)
+    for c in range(PAIR):
+        y_out[pl.ds(c, count, PAIR), :] = result[:, c * LANES : (c + 1) * LANES]
+    exchange(3, y_out, y_in)
+    arrived(3, y_out, y_in, PAIR)
     for block in range(4):
         lanes = pl.ds(block * LANES, LANES)
         convolved = y_in[lanes, :].T
@@ -335,13 +310,14 @@
             *[pltpu.VMEM(c.shape, c.dtype) for c in consts],
             pltpu.VMEM((8, channels), F32),
             pltpu.VMEM((8, channels), F32),
-            *[block] * 13,
+            *[block] * 8,
             wide,
             wide,
             pltpu.VMEM((PAIR * count, 2 * LANES), F32),
             pltpu.SemaphoreType.DMA((7,)),
-            pltpu.SemaphoreType.DMA((7,)),
-            pltpu.SemaphoreType.DMA((7,)),
+            pltpu.SemaphoreType.DMA((5,)),
+            pltpu.SemaphoreType.DMA((5,)),
+            pltpu.SemaphoreType.REGULAR((2,)),
         ],
         compiler_params=pltpu.CompilerParams(
             collective_id=0, has_side_effects=True, vmem_limit_bytes=60 * 1024 * 1024

time: 50 us -> 42.9 us (0.86)
  Pallas kernels: 48.3 us -> 41.1 us
    pallas_call x1, Pallas kernels: 48.3 us -> 41.1 us  [per_device(): pl.pallas_call(functools.partial(kernel, count), out_shape=jax.ShapeDtype...]
where the time goes in v2:
time: 42.9 us; the launch traced here: 42.7 us
  Pallas kernels  41.1 us (96%)
  local copies, waits for them, and re-layouts  1.57 us (4%)
    pallas_call x1, Pallas kernels, per_device(): pl.pallas_call(functools.partial(kernel, count), out_shape=jax.ShapeDtype...  41.1 us
    unnamed x1, local copies, waits for them, and re-layouts  1.57 us

profile of v2, /device:TPU:1, one launch (start us, length us, event | category | flops | bytes accessed | tf_op | source)
XLA Modules:
  0.0 42.7 jit_solution(11171473063704849405)
XLA Ops:
  0.0 41.1 %shard_map.91 = bf16[128,512]{1,0:T(8,128)(2,1)} custom-call(bf16[3,128,512]{2,1,0:T(8,128)(2,1)} %projected.1, f32[3,3,512]{2,1,0:T(4,128)} %taps.1, f32[128,512]{1,0:T(8,128)} %long_filter.1, f32[1,512]{1,0:T(1,128)} %bitcast.1, bf16[2,512,256]{2,1,0:T(8,128)(2,1)} %constant.10.clone.outer_hbm, bf16[2,256,512]{2,1,0:T(8,128)(2,1)} %constant.11.clone.outer_back_hbm, ...), custom_call_target="tpu_custom_call" | custom-call | tf_op jit(solution)/shard_map/pallas_call | solution.py:302
  41.1 1.6 %copy.11 = bf16[128,512]{1,0:T(8,128)(2,1)} copy(bf16[128,512]{1,0:T(8,128)(2,1)} %shard_map.91) | data formatting | bytes 262144

commit v3 on v2

--- a/solution.py
+++ b/solution.py
@@ -16,10 +16,10 @@
 DEPTH = 8
 ROWS = 128
 LANES = 128
+CODE_SCALE = 1.5 * 2.0**20
 PAIR = 2
 GROUP = 8
-BATCH = 15
-STRIDE = 37
+BATCH = 8
 
 
 def halves(table):
@@ -86,6 +86,21 @@
         imags.append(im * twiddle[0] - re * twiddle[1])
     both = jnp.concatenate([jnp.concatenate(reals, axis=1), jnp.concatenate(imags, axis=1)], axis=0)
     return table_times(outer_back, both)
+
+
+def coded(value):
+    power = value * CODE_SCALE
+    for _ in range(3):
+        power = power * power
+    return jnp.where(value < 0, -power, power).astype(BF16)
+
+
+def decoded(code):
+    power = code.astype(F32)
+    size = jnp.abs(power)
+    for _ in range(3):
+        size = jnp.sqrt(size)
+    return jnp.where(power < 0, -size, size) * (1.0 / CODE_SCALE)
 
 
 def kernel(
@@ -113,6 +128,7 @@
     h_z,
     h_mid,
     h_in,
+    h_wide,
     x_out,
     x_in,
     y_out,
@@ -188,11 +204,29 @@
         return pl.ds(pl.multiple_of(device * PAIR, PAIR), PAIR)
 
     def exchange(phase, src, dst):
-        @pl.loop(0, (count - 1) // BATCH)
+        def to(far, near):
+            device = lax.rem(z + far, DEPTH) * plane + lax.rem(p + near, plane)
+            copy(phase, src.at[own_rows(device)], dst.at[own_rows(me)], device).start()
+
+        half = DEPTH // 2
+        batches = plane // BATCH
+
+        @pl.loop(0, batches)
         def _(batch):
-            for step in range(1, BATCH + 1):
-                device = lax.rem(me + (batch * BATCH + step) * STRIDE, count)
-                copy(phase, src.at[own_rows(device)], dst.at[own_rows(me)], device).start()
+            for step in range(BATCH):
+                to(half, plane // 2 + batch * BATCH + step)
+
+        @pl.loop(0, (half - 1) * batches)
+        def _(batch):
+            off = 1 + batch // batches
+            for step in range(BATCH):
+                near = plane // 2 + batch % batches * BATCH + step
+                to(half - off, near)
+                to(half + off, near)
+
+        @pl.loop(1, plane)
+        def _(step):
+            to(0, step)
 
         dst[own_rows(me), :] = src[own_rows(me), :]
 
@@ -205,7 +239,7 @@
     loads[0].wait()
     for block in range(4):
         lanes = pl.ds(block * LANES, LANES)
-        h_out[lanes, :] = filt[:, lanes].T
+        h_out[lanes, :] = coded(filt[:, lanes].T)
 
     loads[1].wait()
     for stream in range(3):
@@ -214,7 +248,7 @@
     rim_out[6:8, :] = jnp.zeros_like(rim_out[6:8, :])
 
     pl.semaphore_wait(barrier, GROUP - 1 + plane // GROUP - 1 + DEPTH - 1 + 2)
-    over_plane(ready.at[0])
+    over_z(ready.at[0])
     rim = copy(0, rim_out, rim_in, right)
     rim.start()
     column = PAIR * plane
@@ -222,13 +256,13 @@
     def piece(index, size):
         return pl.ds(pl.multiple_of(index * size, size), size)
 
-    for step in range(1, DEPTH):
+    for step in (4, 3, 5, 2, 6, 1, 7):
         other = lax.rem(z + step, DEPTH)
         copy(1, h_out.at[piece(other, column)], h_z.at[piece(z, column)], other * plane + p).start()
     h_z[piece(z, column), :] = h_out[piece(z, column), :]
 
-    pl.semaphore_wait(ready.at[0], plane // GROUP - 1)
-    over_z(ready.at[1])
+    pl.semaphore_wait(ready.at[0], DEPTH - 1)
+    over_plane(ready.at[1])
     rim.wait()
 
     row = lax.broadcasted_iota(jnp.int32, (ROWS, 1), 0)
@@ -247,14 +281,15 @@
     for block in range(4):
         lanes = pl.ds(block * LANES, LANES)
         x_out[lanes, :] = mixed[:, lanes].T
-    pl.semaphore_wait(ready.at[1], DEPTH - 1)
+    pl.semaphore_wait(ready.at[1], plane // GROUP - 1)
     exchange(2, x_out, x_in)
 
     arrived(1, h_out, h_z, column)
     part = PAIR * DEPTH
+    h_wide[...] = h_z[...].astype(F32)
     for other in range(plane):
-        for c in range(PAIR):
-            h_mid[pl.ds(other * part + c * DEPTH, DEPTH), :] = h_z[pl.ds(PAIR * other + c, DEPTH, column), :]
+        rows = [h_wide[pl.ds(PAIR * other + c, DEPTH, column), :] for c in range(PAIR)]
+        h_mid[pl.ds(other * part, part), :] = jnp.concatenate(rows, axis=0).astype(BF16)
 
     @pl.loop(1, plane)
     def _(step):
@@ -269,8 +304,9 @@
         load.wait()
 
     arrived(4, h_mid, h_in, part)
+    h_wide[...] = decoded(h_in[...])
     filters = [
-        jnp.concatenate([h_in[pl.ds(c * DEPTH + s, plane, part), :] for s in range(DEPTH)], axis=0)
+        jnp.concatenate([h_wide[pl.ds(c * DEPTH + s, plane, part), :] for s in range(DEPTH)], axis=0)
         for c in range(PAIR)
     ]
     spec_h[...] = spectrum(jnp.concatenate(filters, axis=1), outer, inner, twiddle)
@@ -296,12 +332,13 @@
     channels = long_filter.shape[1]
     outer, outer_back, inner, inner_back, twiddle = consts
     block = pltpu.VMEM((channels, LANES), F32)
+    code = pltpu.VMEM((channels, LANES), BF16)
     wide = pltpu.VMEM((ROWS, channels), F32)
     vmem = pl.BlockSpec(memory_space=pltpu.VMEM)
     anywhere = pl.BlockSpec(memory_space=pl.ANY)
     return pl.pallas_call(
         functools.partial(kernel, count),
-        out_shape=jax.ShapeDtypeStruct((ROWS, channels), BF16),
+        out_shape=pltpu.VMEM((ROWS, channels), BF16),
         in_specs=[anywhere, vmem, anywhere, vmem] + [anywhere] * 5,
         out_specs=vmem,
         scratch_shapes=[
@@ -310,7 +347,8 @@
             *[pltpu.VMEM(c.shape, c.dtype) for c in consts],
             pltpu.VMEM((8, channels), F32),
             pltpu.VMEM((8, channels), F32),
-            *[block] * 8,
+            *[code] * 4,
+            *[block] * 5,
             wide,
             wide,
             pltpu.VMEM((PAIR * count, 2 * LANES), F32),

time: 42.9 us -> 39.3 us (0.916)
  Pallas kernels: 41.1 us -> 38.5 us
  local copies, waits for them, and re-layouts: 1.57 us -> 0.66 us
    pallas_call x1, Pallas kernels: 41.1 us -> 38.5 us  [per_device(): pl.pallas_call(functools.partial(kernel, count), out_shape=pltpu.VMEM((RO...]
    unnamed x1, local copies, waits for them, and re-layouts: 1.57 us -> 0.66 us
where the time goes in v3:
time: 39.3 us; the launch traced here: 39.1 us
  Pallas kernels  38.5 us (98%)
  local copies, waits for them, and re-layouts  0.66 us (2%)
    pallas_call x1, Pallas kernels, per_device(): pl.pallas_call(functools.partial(kernel, count), out_shape=pltpu.VMEM((RO...  38.5 us

profile of v3, /device:TPU:1, one launch (start us, length us, event | category | flops | bytes accessed | tf_op | source)
XLA Modules:
  0.0 39.1 jit_solution(5439319015599201354)
XLA Ops:
  0.0 38.5 %shard_map.91 = bf16[128,512]{1,0:T(8,128)(2,1)S(1)} custom-call(bf16[3,128,512]{2,1,0:T(8,128)(2,1)} %projected.1, f32[3,3,512]{2,1,0:T(4,128)} %taps.1, f32[128,512]{1,0:T(8,128)} %long_filter.1, f32[1,512]{1,0:T(1,128)} %bitcast.1, bf16[2,512,256]{2,1,0:T(8,128)(2,1)} %constant.10.clone.outer_hbm, bf16[2,256,512]{2,1,0:T(8,128)(2,1)} %constant.11.clone.outer_back_hbm, ...), custom_call_target="tpu_custom_call" | custom-call | tf_op jit(solution)/shard_map/pallas_call | solution.py:339
  38.5 0.7 %copy.11 = bf16[128,512]{1,0:T(8,128)(2,1)} copy(bf16[128,512]{1,0:T(8,128)(2,1)S(1)} %shard_map.91) | data formatting | bytes 262144

commit v4 on v3

--- a/solution.py
+++ b/solution.py
@@ -16,9 +16,9 @@
 DEPTH = 8
 ROWS = 128
 LANES = 128
+CODE_LIMIT = 1.4 * 2.0**15
 CODE_SCALE = 1.5 * 2.0**20
 PAIR = 2
-GROUP = 8
 BATCH = 8
 
 
@@ -89,7 +89,7 @@
 
 
 def coded(value):
-    power = value * CODE_SCALE
+    power = value
     for _ in range(3):
         power = power * power
     return jnp.where(value < 0, -power, power).astype(BF16)
@@ -100,7 +100,7 @@
     size = jnp.abs(power)
     for _ in range(3):
         size = jnp.sqrt(size)
-    return jnp.where(power < 0, -size, size) * (1.0 / CODE_SCALE)
+    return jnp.where(power < 0, -size, size)
 
 
 def kernel(
@@ -131,6 +131,10 @@
     h_wide,
     x_out,
     x_in,
+    size_out,
+    size_z,
+    size_in,
+    y_wide,
     y_out,
     y_in,
     mixed,
@@ -145,7 +149,6 @@
     plane = count // DEPTH
     z = me // plane
     p = me % plane
-    unit = me % GROUP
     right = (me + 1) % count
     left = (me + count - 1) % count
 
@@ -170,14 +173,6 @@
     def signal(semaphore, device):
         pl.semaphore_signal(semaphore, inc=1, device_id=(device,), device_id_type=MESH)
 
-    def over_group(semaphore):
-        for step in range(1, GROUP):
-            signal(semaphore, me - unit + lax.rem(unit + step, GROUP))
-
-    def over_plane(semaphore):
-        for step in range(1, plane // GROUP):
-            signal(semaphore, z * plane + lax.rem(p + step * GROUP, plane))
-
     def over_z(semaphore):
         for step in range(1, DEPTH):
             signal(semaphore, lax.rem(me + step * plane, count))
@@ -185,8 +180,8 @@
     over_z(barrier)
     signal(barrier, right)
     signal(barrier, left)
-    over_plane(barrier)
-    over_group(barrier)
+    for step in range(1, plane):
+        signal(barrier, z * plane + lax.rem(p + step, plane))
     for load in loads[1:]:
         load.start()
 
@@ -203,7 +198,7 @@
     def own_rows(device):
         return pl.ds(pl.multiple_of(device * PAIR, PAIR), PAIR)
 
-    def exchange(phase, src, dst):
+    def exchange(phase, src, dst, between=None):
         def to(far, near):
             device = lax.rem(z + far, DEPTH) * plane + lax.rem(p + near, plane)
             copy(phase, src.at[own_rows(device)], dst.at[own_rows(me)], device).start()
@@ -216,22 +211,28 @@
             for step in range(BATCH):
                 to(half, plane // 2 + batch * BATCH + step)
 
-        @pl.loop(0, (half - 1) * batches)
-        def _(batch):
+        def around(batch):
             off = 1 + batch // batches
             for step in range(BATCH):
                 near = plane // 2 + batch % batches * BATCH + step
                 to(half - off, near)
                 to(half + off, near)
 
+        pl.loop(0, batches)(around)
+        if between is not None:
+            between()
+        pl.loop(batches, (half - 1) * batches)(around)
+
         @pl.loop(1, plane)
         def _(step):
             to(0, step)
 
-        dst[own_rows(me), :] = src[own_rows(me), :]
+        own = pltpu.make_async_copy(src.at[own_rows(me)], dst.at[own_rows(me)], load_sem.at[7])
+        own.start()
+        own.wait()
 
     def arrived(phase, src, dst, own):
-        rows = pl.ds(0, PAIR * count - own)
+        rows = pl.ds(0, dst.shape[0] - own)
         done = copy(phase, src.at[rows], dst.at[rows], right)
         done.wait_send()
         done.wait_recv()
@@ -239,7 +240,7 @@
     loads[0].wait()
     for block in range(4):
         lanes = pl.ds(block * LANES, LANES)
-        h_out[lanes, :] = coded(filt[:, lanes].T)
+        h_out[lanes, :] = coded(filt[:, lanes].T * CODE_SCALE)
 
     loads[1].wait()
     for stream in range(3):
@@ -247,8 +248,8 @@
         rim_out[2 * stream : 2 * stream + 2, :] = tail[14:16, :]
     rim_out[6:8, :] = jnp.zeros_like(rim_out[6:8, :])
 
-    pl.semaphore_wait(barrier, GROUP - 1 + plane // GROUP - 1 + DEPTH - 1 + 2)
-    over_z(ready.at[0])
+    pl.semaphore_wait(barrier, plane - 1 + DEPTH - 1 + 2)
+    over_z(ready)
     rim = copy(0, rim_out, rim_in, right)
     rim.start()
     column = PAIR * plane
@@ -261,8 +262,6 @@
         copy(1, h_out.at[piece(other, column)], h_z.at[piece(z, column)], other * plane + p).start()
     h_z[piece(z, column), :] = h_out[piece(z, column), :]
 
-    pl.semaphore_wait(ready.at[0], DEPTH - 1)
-    over_plane(ready.at[1])
     rim.wait()
 
     row = lax.broadcasted_iota(jnp.int32, (ROWS, 1), 0)
@@ -278,25 +277,46 @@
         )
 
     mixed[...] = short(1) * short(2)
+
+    def energy(ref):
+        return jnp.sum(ref[...] * ref[...], axis=(0, 1), keepdims=True)
+
+    lane = lax.broadcasted_iota(jnp.int32, size_out.shape, 1)
+    size_out[...] = jnp.where(lane < LANES // 2, energy(mixed), energy(filt))
+    for step in range(1, DEPTH):
+        to = lax.rem(z + step, DEPTH) * plane + p
+        copy(5, size_out.at[pl.ds(0, 1)], size_z.at[pl.ds(z, 1)], to).start()
+    size_z[pl.ds(z, 1), :] = size_out[0:1, :]
     for block in range(4):
         lanes = pl.ds(block * LANES, LANES)
         x_out[lanes, :] = mixed[:, lanes].T
-    pl.semaphore_wait(ready.at[1], plane // GROUP - 1)
-    exchange(2, x_out, x_in)
-
-    arrived(1, h_out, h_z, column)
+    pl.semaphore_wait(ready, DEPTH - 1)
     part = PAIR * DEPTH
-    h_wide[...] = h_z[...].astype(F32)
-    for other in range(plane):
-        rows = [h_wide[pl.ds(PAIR * other + c, DEPTH, column), :] for c in range(PAIR)]
-        h_mid[pl.ds(other * part, part), :] = jnp.concatenate(rows, axis=0).astype(BF16)
+
+    def filter_in_plane():
+        arrived(1, h_out, h_z, column)
+        h_wide[...] = h_z[...].astype(F32)
+        for other in range(plane):
+            rows = [h_wide[pl.ds(PAIR * other + c, DEPTH, column), :] for c in range(PAIR)]
+            h_mid[pl.ds(other * part, part), :] = jnp.concatenate(rows, axis=0).astype(BF16)
+
+        @pl.loop(1, plane)
+        def _(step):
+            other = lax.rem(p + step, plane)
+            copy(4, h_mid.at[piece(other, part)], h_in.at[piece(p, part)], z * plane + other).start()
+
+        h_in[piece(p, part), :] = h_mid[piece(p, part), :]
+
+    exchange(2, x_out, x_in, filter_in_plane)
+
+    arrived(5, size_z, size_z, 1)
 
     @pl.loop(1, plane)
     def _(step):
-        other = lax.rem(p + step, plane)
-        copy(4, h_mid.at[piece(other, part)], h_in.at[piece(p, part)], z * plane + other).start()
-
-    h_in[piece(p, part), :] = h_mid[piece(p, part), :]
+        device = z * plane + lax.rem(p + step, plane)
+        copy(6, size_z, size_in.at[piece(p, DEPTH)], device).start()
+
+    size_in[piece(p, DEPTH), :] = size_z[...]
 
     query[...] = short(0)
     mixed[...] = skip[...] * mixed[...]
@@ -304,7 +324,7 @@
         load.wait()
 
     arrived(4, h_mid, h_in, part)
-    h_wide[...] = decoded(h_in[...])
+    h_wide[...] = decoded(h_in[...]) * (1.0 / CODE_SCALE)
     filters = [
         jnp.concatenate([h_wide[pl.ds(c * DEPTH + s, plane, part), :] for s in range(DEPTH)], axis=0)
         for c in range(PAIR)
@@ -319,12 +339,16 @@
     product = jnp.concatenate([xr * hr - xi * hi, xr * hi + xi * hr], axis=1)
     result = signal_of(product, outer_back, inner_back, twiddle)
     for c in range(PAIR):
-        y_out[pl.ds(c, count, PAIR), :] = result[:, c * LANES : (c + 1) * LANES]
+        y_wide[pl.ds(c, count, PAIR), :] = result[:, c * LANES : (c + 1) * LANES]
+    arrived(6, size_in, size_in, DEPTH)
+    total = jnp.sum(size_in[...], axis=0, keepdims=True)
+    reach = jnp.maximum(jnp.sqrt(total[:, :1]) * jnp.sqrt(total[:, LANES // 2 : LANES // 2 + 1]), 1e-12)
+    y_out[...] = coded(y_wide[...] * (CODE_LIMIT / reach))
     exchange(3, y_out, y_in)
     arrived(3, y_out, y_in, PAIR)
     for block in range(4):
         lanes = pl.ds(block * LANES, LANES)
-        convolved = y_in[lanes, :].T
+        convolved = (decoded(y_in[lanes, :]) * (reach * (1.0 / CODE_LIMIT))).T
         gated[:, lanes] = (query[:, lanes] * (convolved + mixed[:, lanes])).astype(BF16)
 
 
@@ -348,14 +372,19 @@
             pltpu.VMEM((8, channels), F32),
             pltpu.VMEM((8, channels), F32),
             *[code] * 4,
-            *[block] * 5,
+            *[block] * 3,
+            pltpu.VMEM((8, LANES), F32),
+            pltpu.VMEM((DEPTH, LANES), F32),
+            pltpu.VMEM((count, LANES), F32),
+            block,
+            *[code] * 2,
             wide,
             wide,
             pltpu.VMEM((PAIR * count, 2 * LANES), F32),
+            pltpu.SemaphoreType.DMA((8,)),
             pltpu.SemaphoreType.DMA((7,)),
-            pltpu.SemaphoreType.DMA((5,)),
-            pltpu.SemaphoreType.DMA((5,)),
-            pltpu.SemaphoreType.REGULAR((2,)),
+            pltpu.SemaphoreType.DMA((7,)),
+            pltpu.SemaphoreType.REGULAR,
         ],
         compiler_params=pltpu.CompilerParams(
             collective_id=0, has_side_effects=True, vmem_limit_bytes=60 * 1024 * 1024

time: 39.3 us -> 37.8 us (0.962)
  Pallas kernels: 38.5 us -> 37 us
    pallas_call x1, Pallas kernels: 38.5 us -> 37 us  [per_device(): pl.pallas_call(functools.partial(kernel, count), out_shape=pltpu.VMEM((RO...]
where the time goes in v4:
time: 37.8 us; the launch traced here: 37.6 us
  Pallas kernels  37 us (98%)
  local copies, waits for them, and re-layouts  0.66 us (2%)
    pallas_call x1, Pallas kernels, per_device(): pl.pallas_call(functools.partial(kernel, count), out_shape=pltpu.VMEM((RO...  37 us

profile of v4, /device:TPU:1, one launch (start us, length us, event | category | flops | bytes accessed | tf_op | source)
XLA Modules:
  0.0 37.6 jit_solution(10410772892970184312)
XLA Ops:
  0.0 37.0 %shard_map.91 = bf16[128,512]{1,0:T(8,128)(2,1)S(1)} custom-call(bf16[3,128,512]{2,1,0:T(8,128)(2,1)} %projected.1, f32[3,3,512]{2,1,0:T(4,128)} %taps.1, f32[128,512]{1,0:T(8,128)} %long_filter.1, f32[1,512]{1,0:T(1,128)} %bitcast.1, bf16[2,512,256]{2,1,0:T(8,128)(2,1)} %constant.10.clone.outer_hbm, bf16[2,256,512]{2,1,0:T(8,128)(2,1)} %constant.11.clone.outer_back_hbm, ...), custom_call_target="tpu_custom_call" | custom-call | tf_op jit(solution)/shard_map/pallas_call | solution.py:363
  37.0 0.7 %copy.11 = bf16[128,512]{1,0:T(8,128)(2,1)} copy(bf16[128,512]{1,0:T(8,128)(2,1)S(1)} %shard_map.91) | data formatting | bytes 262144

commit v5 on v4

--- a/solution.py
+++ b/solution.py
@@ -218,10 +218,9 @@
                 to(half - off, near)
                 to(half + off, near)
 
-        pl.loop(0, batches)(around)
+        pl.loop(0, (half - 1) * batches)(around)
         if between is not None:
             between()
-        pl.loop(batches, (half - 1) * batches)(around)
 
         @pl.loop(1, plane)
         def _(step):

time: 37.8 us -> 37.1 us (0.981)
  Pallas kernels: 37 us -> 36.3 us
    pallas_call x1, Pallas kernels: 37 us -> 36.3 us  [per_device(): pl.pallas_call(functools.partial(kernel, count), out_shape=pltpu.VMEM((RO...]
where the time goes in v5:
time: 37.1 us; the launch traced here: 37 us
  Pallas kernels  36.3 us (98%)
  local copies, waits for them, and re-layouts  0.66 us (2%)
    pallas_call x1, Pallas kernels, per_device(): pl.pallas_call(functools.partial(kernel, count), out_shape=pltpu.VMEM((RO...  36.3 us

profile of v5, /device:TPU:1, one launch (start us, length us, event | category | flops | bytes accessed | tf_op | source)
XLA Modules:
  0.0 37.0 jit_solution(10321173191616150265)
XLA Ops:
  0.0 36.3 %shard_map.91 = bf16[128,512]{1,0:T(8,128)(2,1)S(1)} custom-call(bf16[3,128,512]{2,1,0:T(8,128)(2,1)} %projected.1, f32[3,3,512]{2,1,0:T(4,128)} %taps.1, f32[128,512]{1,0:T(8,128)} %long_filter.1, f32[1,512]{1,0:T(1,128)} %bitcast.1, bf16[2,512,256]{2,1,0:T(8,128)(2,1)} %constant.10.clone.outer_hbm, bf16[2,256,512]{2,1,0:T(8,128)(2,1)} %constant.11.clone.outer_back_hbm, ...), custom_call_target="tpu_custom_call" | custom-call | tf_op jit(solution)/shard_map/pallas_call | solution.py:362
  36.3 0.7 %copy.11 = bf16[128,512]{1,0:T(8,128)(2,1)} copy(bf16[128,512]{1,0:T(8,128)(2,1)S(1)} %shard_map.91) | data formatting | bytes 262144
